TPU v7x, 32 devices: a whole 2x2x4 slice. The times are simulated.
32 devices in a mesh: dp: 4 (over z), tile: 4 (over x, core), seq: 2 (over y).
Axes of the slice: x: 2, y: 2, z: 4, core: 2. Of those that a mesh axis runs over, the one named last changes fastest.
Arguments:
- features: bfloat16 [4, 8, 16, 32, 128], P('dp', None, 'tile'), may hold values from -6 to 6
- lengths: int32 [4], P('dp'), may hold values from 1 to 8, as said below
- weight: bfloat16 [3456, 5120], P(('dp', 'tile'), 'seq'), may hold values from -0.109375 to 0.109375
- bias: bfloat16 [5120], P('seq'), may hold values from -3 to 3
- cotangent: bfloat16 [4, 8, 16, 32, 5120], P('dp', 'seq', 'tile'), may hold values from -6 to 6
Outputs:
- pose_tokens: bfloat16 [4, 8, 16, 32, 5120], P('dp', 'seq', 'tile')
- grad_features: bfloat16 [4, 8, 16, 32, 128], P('dp', None, 'tile')
- grad_weight: float32 [3456, 5120], P(('dp', 'tile'), 'seq')
- grad_bias: float32 [5120], P('seq')
Inputs may be any that keep to these rules, and one draw needn't show every extreme that they name: `lengths`: exactly one clip has 8 live frames; every other clip has at most 4.
All inputs are finite; a program needn't handle non-finite values.
Results may differ from a plain program's by a relative error of at most 0.005.
Values may be sent and summed in bfloat16 or wider, within the bound.
A program may use at most 512 MiB of HBM per device.

v0:
```python
import jax
import jax.numpy as jnp
from jax import lax
from jax.sharding import PartitionSpec as P


def pick(pieces, index):
    result = pieces[0]
    for place in range(1, len(pieces)):
        result = jnp.where(index == place, pieces[place], result)
    return result


def swap(value, axis, distance):
    count = lax.axis_size(axis)
    return lax.ppermute(value, axis, [(i, i ^ distance) for i in range(count)])


def sum_over(value, axes):
    for axis in axes:
        distance = 1
        while distance < lax.axis_size(axis):
            value = value + swap(value, axis, distance)
            distance *= 2
    return value


def exchange(parts, axis):
    me = lax.axis_index(axis)
    count = lax.axis_size(axis)
    by_offset = [pick(parts, me)]
    for offset in range(1, count):
        by_offset.append(swap(pick(parts, me ^ offset), axis, offset))
    return [pick(by_offset, me ^ source) for source in range(count)]


def neighbours(low_row, high_row, axis):
    count = lax.axis_size(axis)
    forward = [(i, i + 1) for i in range(count - 1)]
    backward = [(i + 1, i) for i in range(count - 1)]
    return (lax.ppermute(high_row, axis, forward), lax.ppermute(low_row, axis, backward))


def silu_grad(values):
    sigma = jax.nn.sigmoid(values)
    return sigma * (1.0 + values * (1.0 - sigma))


def shards(features, lengths, weight, bias, cotangent):
    seq_count = lax.axis_size("seq")
    local_feat = features[0]
    frame_count, row_count, col_count, chan_count = local_feat.shape
    row_total = frame_count * row_count * col_count
    share = weight.shape[1]
    frame_share = frame_count // seq_count
    frame_mask = (jnp.arange(frame_count) < lengths[0]).astype(jnp.float32)[:, None, None, None]
    cot = cotangent[0]
    received = exchange([cot[..., j * share : (j + 1) * share] for j in range(seq_count)], "seq")
    grad_out = jnp.concatenate(received, axis=0) * frame_mask.astype(jnp.bfloat16)
    flat_grad = grad_out.reshape(row_total, share)
    inner_vals = local_feat.astype(jnp.float32)
    hidden = (jax.nn.silu(inner_vals) * frame_mask).astype(jnp.bfloat16)
    above, below = neighbours(hidden[:, :1], hidden[:, -1:], "tile")
    padded = jnp.pad(
        jnp.concatenate([above, hidden, below], axis=1), ((1, 1), (0, 0), (1, 1), (0, 0))
    )
    wide = jnp.concatenate([padded[:, :, e : e + col_count] for e in range(3)], axis=3)
    columns = jnp.concatenate(
        [wide[a : a + frame_count, b : b + row_count] for a in range(3) for b in range(3)], axis=3
    ).reshape(row_total, 27 * chan_count)
    weight_term = lax.dot_general(
        columns, flat_grad, (((0,), (0,)), ((), ())), preferred_element_type=jnp.float32
    ).astype(jnp.bfloat16)
    grad_weight = lax.psum_scatter(
        weight_term, ("dp", "tile"), scatter_dimension=0, tiled=True
    ).astype(jnp.float32)
    grad_bias = sum_over(jnp.sum(flat_grad, axis=0, dtype=jnp.float32), ("tile", "dp"))
    full_weight = lax.all_gather(weight, ("dp", "tile"), axis=0, tiled=True)
    output = jnp.dot(columns, full_weight, preferred_element_type=jnp.float32)
    tokens = (
        (output.reshape(frame_count, row_count, col_count, share) + bias.astype(jnp.float32))
        * frame_mask
    ).astype(jnp.bfloat16)
    pose_tokens = jnp.concatenate(
        exchange(
            [tokens[j * frame_share : (j + 1) * frame_share] for j in range(seq_count)], "seq"
        ),
        axis=3,
    )
    spread = lax.dot_general(
        flat_grad, full_weight, (((1,), (1,)), ((), ())), preferred_element_type=jnp.float32
    ).reshape(frame_count, row_count, col_count, 27 * chan_count)
    total = jnp.zeros((frame_count, row_count + 2, col_count, chan_count), jnp.float32)
    for a in range(3):
        for b in range(3):
            start = (a * 3 + b) * 3 * chan_count
            first = spread[..., start : start + chan_count]
            second = spread[..., start + chan_count : start + 2 * chan_count]
            third = spread[..., start + 2 * chan_count : start + 3 * chan_count]
            none = ((0, 0), (0, 0))
            joined = (
                jnp.pad(first[:, :, 1:], (*none, (0, 1), (0, 0)))
                + second
                + jnp.pad(third[:, :, :-1], (*none, (1, 0), (0, 0)))
            )
            kept = joined[max(0, 1 - a) : frame_count - max(0, a - 1)]
            total = total + jnp.pad(
                kept, ((max(0, a - 1), max(0, 1 - a)), (b, 2 - b), (0, 0), (0, 0))
            )
    from_above, from_below = neighbours(total[:, :1], total[:, -1:], "tile")
    rims = jnp.concatenate([from_above, jnp.zeros_like(total[:, 2:-2]), from_below], axis=1)
    grad_hidden = sum_over(total[:, 1:-1] + rims, ("seq",))
    grad_features = (silu_grad(inner_vals) * grad_hidden * frame_mask).astype(jnp.bfloat16)
    return (pose_tokens[None], grad_features[None], grad_weight, grad_bias)


def solution(mesh):
    return jax.shard_map(
        shards,
        mesh=mesh,
        in_specs=(
            P("dp", None, "tile", None, None),
            P("dp"),
            P(("dp", "tile"), "seq"),
            P("seq"),
            P("dp", "seq", "tile", None, None),
        ),
        out_specs=(
            P("dp", "seq", "tile", None, None),
            P("dp", None, "tile", None, None),
            P(("dp", "tile"), "seq"),
            P("seq"),
        ),
        check_vma=False,
    )
```

profile of v0, /device:TPU:0, one launch (start us, length us, event | category | flops | bytes accessed | tf_op | source)
XLA Modules:
  0.0 396.1 jit_solution(2411242803760982149)
XLA Ops:
  7.2 0.0 all-gather.2.cloned.1.call-start
  7.2 0.7 all-gather.2.cloned.1.call-update
  7.9 0.0 reduce-scatter.2.cloned.1.call-start
  8.0 2.8 broadcast_select_fusion.1
  10.8 3.0 collective-permute-start.3
  14.5 56.3 %collective-permute-done.3 = bf16[4,4,32,2560]{3,2,1,0:T(8,128)(2,1)} collective-permute-done((bf16[4,4,32,2560]{3,2,1,0:T(8,128)(2,1)S(1)}, bf16[4,4,32,2560]{3,2,1,0:T(8,128)(2,1)}, u32[]{:S(2)}, u32[]{:S(2)}) %collective-permute-start.3) | collective-permute-done | bytes 2621472 | tf_op jit(solution)/shard_map/ppermute | solution.py:16
  70.8 5.0 %broadcast_select_fusion.4 = (bf16[4,4,32,2560]{3,2,1,0:T(8,128)(2,1)S(1)}, bf16[4,4,32,2560]{3,2,1,0:T(8,128)(2,1)}) fusion(bf16[4,4,32,2560]{3,2,1,0:T(8,128)(2,1)} %collective-permute-done.3, pred[]{:T(512)S(6)} %eq.4, bf16[4,4,32,5120]{3,2,1,0:T(8,128)(2,1)} %bitcast.30, pred[]{:T(512)S(6)} %eq.5), kind=kLoop, calls=%fused_computation.13 | loop fusion | flops 3932160 | bytes 13107202 | tf_op jit(solution)/shard_map/jit(_where)/select_n | solution.py:10
  75.8 29.9 %all-gather.2.cloned.1.call-done = bf16[3456,2560]{1,0:T(8,128)(2,1)} async-done(((bf16[216,2560]{1,0:T(8,128)(2,1)}), bf16[3456,2560]{1,0:T(8,128)(2,1)}) %all-gather.2.cloned.1.call-update) | async-done | bytes 17694736 | tf_op jit(solution)/shard_map/all_gather | solution.py:78
  105.7 26.6 %fusion = f32[8,4,32,3456]{3,2,1,0:T(8,128)} fusion(bf16[3456,2560]{1,0:T(8,128)(2,1)} %all-gather.2.cloned.1.call-done, bf16[4,4,32,2560]{3,2,1,0:T(8,128)(2,1)} %get-tuple-element.32, bf16[4,4,32,2560]{3,2,1,0:T(8,128)(2,1)S(1)} %get-tuple-element.31, bf16[8]{0:T(256)(128)(2,1)S(1)} %fusion.26), kind=kOutput, calls=%fused_computation.1 | convolution fusion | flops 18124636160 | bytes 37093392 | tf_op jit(solution)/shard_map/dot_general | solution.py:90
  132.3 5.1 %fusion.27 = (f32[8,4,31,128]{3,2,1,0:T(8,128)S(1)}, f32[8,4,31,128]{3,2,1,0:T(8,128)S(1)}, f32[8,4,31,128]{3,2,1,0:T(8,128)S(1)}, f32[8,4,31,128]{3,2,1,0:T(8,1...) fusion(f32[8,4,32,3456]{3,2,1,0:T(8,128)} %fusion), kind=kLoop, calls=%fused_computation.75 | loop fusion | bytes 18284544 | tf_op jit(solution)/shard_map/slice | solution.py:102
  137.4 3.5 fusion.28
  140.8 0.4 pad_add_fusion.1
  141.2 0.4 pad_add_fusion.3
  141.6 0.0 copy-start.2
  141.6 0.4 pad_add_fusion.5
  141.9 0.5 pad_add_fusion
  142.5 1.3 collective-permute-start.5
  143.8 3.0 collective-permute-start.4
  146.8 0.1 pad.125.clone
  146.9 0.9 collective-permute-done.4
  147.8 0.1 slice_add_fusion
  147.9 1.6 collective-permute-start.6
  149.5 11.7 %collective-permute-done.6 = f32[8,4,32,128]{3,2,1,0:T(8,128)S(1)} collective-permute-done((f32[8,4,32,128]{3,2,1,0:T(8,128)S(1)}, f32[8,4,32,128]{3,2,1,0:T(8,128)S(1)}, u32[]{:S(2)}, u32[]{:S(2)}) %collective-permute-start.6) | collective-permute-done | bytes 524320 | tf_op jit(solution)/shard_map/ppermute | solution.py:16
  161.2 1.0 fusion.25
  162.3 1.3 collective-permute-start.1
  163.6 4.1 %collective-permute-start = (bf16[8,1,32,128]{3,2,1,0:T(8,128)(2,1)S(1)}, bf16[8,1,32,128]{3,2,1,0:T(8,128)(2,1)S(1)}, u32[]{:S(2)}, u32[]{:S(2)}) collective-permute-start(bf16[8,1,32,128]{3,2,1,0:T(8,128)(2,1)S(1)} %get-tuple-element.42), channel_id=1, source_target_pairs={{0,2},{2,4},{4,6},{1,3},{3,5},{5,7},{8,10},{10,12},{12,14},{9,11},... | collective-permute-start | bytes 196616 | tf_op jit(solution)/shard_map/ppermute | solution.py:41
  167.7 0.7 collective-permute-done
  168.4 0.2 select_maximum_fusion
  168.6 0.3 fusion.30
  168.9 0.2 pad_maximum_fusion
  169.2 0.1 slice_dynamic-update-slice_fusion.8
  169.3 0.1 slice_dynamic-update-slice_fusion.7
  169.4 0.0 copy-start
  169.4 0.1 slice_dynamic-update-slice_fusion.6
  169.6 0.1 slice_dynamic-update-slice_fusion.5
  169.7 0.1 slice_dynamic-update-slice_fusion.4
  169.9 0.1 slice_dynamic-update-slice_fusion.3
  170.0 0.1 slice_dynamic-update-slice_fusion.2
  170.2 0.1 slice_dynamic-update-slice_fusion.1
  170.4 0.1 slice_dynamic-update-slice_fusion
  170.5 2.9 copy-done.3
  173.4 21.5 %bitcast_convert_fusion = bf16[3456,2560]{1,0:T(8,128)(2,1)} fusion(bf16[8,4,32,3456]{3,2,1,0:T(8,128)(2,1)S(1)} %slice_dynamic-update-slice_fusion, bf16[4,4,32,2560]{3,2,1,0:T(8,128)(2,1)S(1)} %copy-done, bf16[4,4,32,2560]{3,2,1,0:T(8,128)(2,1)S(1)} %get-tuple-element.31, bf16[8]{0:T(256)(128)(2,1)S(1)} %fusion.26), kind=kOutput, calls=%fused_computation | convolution fusion | flops 18133483520 | bytes 30015504 | tf_op jit(solution)/shard_map/dot_general | solution.py:71
  194.9 0.0 reduce-scatter.2.cloned.1.call-update
  194.9 0.7 copy-done.4
  195.6 23.9 %multiply_convert_fusion = bf16[8,4,32,2560]{3,2,1,0:T(8,128)(2,1)S(1)} fusion(bf16[8,4,32,3456]{3,2,1,0:T(8,128)(2,1)} %copy-done.3, bf16[3456,2560]{1,0:T(8,128)(2,1)} %all-gather.2.cloned.1.call-done, f32[8]{0:T(128)S(1)} %copy-done.6, f32[2560]{0:T(1024)S(1)} %convert_element_type.90), kind=kOutput, calls=%fused_computation.6 | convolution fusion | flops 18127257600 | bytes 30025760 | tf_op jit(solution)/shard_map/dot_general | solution.py:79
  219.5 0.0 copy-start.1
  219.5 0.3 broadcast_select_fusion.3
  219.8 1.6 collective-permute-start.2
  221.4 0.3 copy-done.1
  221.7 1.5 convert_reduce_fusion
  223.3 2.2 collective-permute-start.7
  225.5 0.8 collective-permute-done.7
  226.3 2.6 collective-permute-start.8
  228.9 1.7 collective-permute-done.8
  230.6 1.5 collective-permute-start.9
  232.1 2.2 collective-permute-done.9
  234.3 2.4 collective-permute-start.10
  236.7 2.3 collective-permute-done.10
  239.0 0.6 add.205
  239.6 38.8 %collective-permute-done.2 = bf16[4,4,32,2560]{3,2,1,0:T(8,128)(2,1)S(1)} collective-permute-done((bf16[4,4,32,2560]{3,2,1,0:T(8,128)(2,1)S(1)}, bf16[4,4,32,2560]{3,2,1,0:T(8,128)(2,1)S(1)}, u32[]{:S(2)}, u32[]{:S(2)}) %collective-permute-start.2) | collective-permute-done | bytes 2621472 | tf_op jit(solution)/shard_map/ppermute | solution.py:16
  278.4 0.5 broadcast_select_fusion.6
  278.9 3.0 maximum_bitcast_fusion
  281.9 104.5 %reduce-scatter.2.cloned.1.call-done = bf16[216,2560]{1,0:T(8,128)(2,1)} async-done(((bf16[3456,2560]{1,0:T(8,128)(2,1)}), bf16[216,2560]{1,0:T(8,128)(2,1)}) %reduce-scatter.2.cloned.1.call-update) | async-done | bytes 1105936 | tf_op jit(solution)/shard_map/reduce_scatter | solution.py:74
  386.4 2.9 convert_element_type.95
  (19 shorter events, 0.1 us)
Async XLA Ops:
  7.2 98.6 %all-gather.2.cloned.1.call-start = ((), (), s32[]{:S(2)}) async-start(), calls=%async_computation.1 | async-start | bytes 18800640 | tf_op jit(solution)/shard_map/all_gather | solution.py:78
  7.9 378.5 %reduce-scatter.2.cloned.1.call-start = ((), (), s32[]{:S(2)}) async-start(), calls=%async_computation.2 | async-start | bytes 18800640 | tf_op jit(solution)/shard_map/reduce_scatter | solution.py:74
  10.8 60.0 %collective-permute-start.3 = (bf16[4,4,32,2560]{3,2,1,0:T(8,128)(2,1)S(1)}, bf16[4,4,32,2560]{3,2,1,0:T(8,128)(2,1)}, u32[]{:S(2)}, u32[]{:S(2)}) collective-permute-start(bf16[4,4,32,2560]{3,2,1,0:T(8,128)(2,1)S(1)} %broadcast_select_fusion.1), channel_id=1, source_target_pairs={{0,1},{1,0},{2,3},{3,2},{4,5},{5,4},{6,7},{7,6},{8,9},{9,8},{10,11... | collective-permute-start | bytes 7864328 | tf_op jit(solution)/shard_map/ppermute | solution.py:16
  141.6 19.7 %copy-start.2 = (bf16[1,8,4,32,128]{4,3,2,1,0:T(8,128)(2,1)S(1)}, bf16[1,8,4,32,128]{4,3,2,1,0:T(8,128)(2,1)}, u32[]{:S(2)}) copy-start(bf16[1,8,4,32,128]{4,3,2,1,0:T(8,128)(2,1)} %param.5) | copy-start | bytes 786436
  142.5 4.4 %collective-permute-start.5 = (f32[8,1,32,128]{3,2,1,0:T(8,128)S(1)}, f32[8,1,32,128]{3,2,1,0:T(8,128)S(1)}, u32[]{:S(2)}, u32[]{:S(2)}) collective-permute-start(f32[8,1,32,128]{3,2,1,0:T(8,128)S(1)} %get-tuple-element.36), channel_id=1, source_target_pairs={{2,0},{4,2},{6,4},{3,1},{5,3},{7,5},{10,8},{12,10},{14,12},{11,9},... | collective-permute-start | bytes 393224 | tf_op jit(solution)/shard_map/ppermute | solution.py:41
  143.8 4.0 %collective-permute-start.4 = (f32[8,1,32,128]{3,2,1,0:T(8,128)S(1)}, f32[8,1,32,128]{3,2,1,0:T(8,128)S(1)}, u32[]{:S(2)}, u32[]{:S(2)}) collective-permute-start(f32[8,1,32,128]{3,2,1,0:T(8,128)S(1)} %get-tuple-element.35), channel_id=1, source_target_pairs={{0,2},{2,4},{4,6},{1,3},{3,5},{5,7},{8,10},{10,12},{12,14},{9,11},... | collective-permute-start | bytes 393224 | tf_op jit(solution)/shard_map/ppermute | solution.py:41
  147.9 13.3 %collective-permute-start.6 = (f32[8,4,32,128]{3,2,1,0:T(8,128)S(1)}, f32[8,4,32,128]{3,2,1,0:T(8,128)S(1)}, u32[]{:S(2)}, u32[]{:S(2)}) collective-permute-start(f32[8,4,32,128]{3,2,1,0:T(8,128)S(1)} %slice_add_fusion), channel_id=1, source_target_pairs={{0,1},{1,0},{2,3},{3,2},{4,5},{5,4},{6,7},{7,6},{8,9},{9,8},{10,11... | collective-permute-start | bytes 1572872 | tf_op jit(solution)/shard_map/ppermute | solution.py:16
  149.5 19.7 %copy-start.5 = (f32[8]{0:T(128)}, f32[8]{0:T(128)S(1)}, u32[]{:S(2)}) copy-start(f32[8]{0:T(128)S(1)} %compare_convert_fusion) | copy-start | bytes 100
  162.3 5.4 %collective-permute-start.1 = (bf16[8,1,32,128]{3,2,1,0:T(8,128)(2,1)S(1)}, bf16[8,1,32,128]{3,2,1,0:T(8,128)(2,1)S(1)}, u32[]{:S(2)}, u32[]{:S(2)}) collective-permute-start(bf16[8,1,32,128]{3,2,1,0:T(8,128)(2,1)S(1)} %get-tuple-element.43), channel_id=1, source_target_pairs={{2,0},{4,2},{6,4},{3,1},{5,3},{7,5},{10,8},{12,10},{14,12},{11,9},... | collective-permute-start | bytes 196616 | tf_op jit(solution)/shard_map/ppermute | solution.py:41
  163.6 4.8 %collective-permute-start = (bf16[8,1,32,128]{3,2,1,0:T(8,128)(2,1)S(1)}, bf16[8,1,32,128]{3,2,1,0:T(8,128)(2,1)S(1)}, u32[]{:S(2)}, u32[]{:S(2)}) collective-permute-start(bf16[8,1,32,128]{3,2,1,0:T(8,128)(2,1)S(1)} %get-tuple-element.42), channel_id=1, source_target_pairs={{0,2},{2,4},{4,6},{1,3},{3,5},{5,7},{8,10},{10,12},{12,14},{9,11},... | collective-permute-start | bytes 196616 | tf_op jit(solution)/shard_map/ppermute | solution.py:41
  169.4 4.0 %copy-start = (bf16[4,4,32,2560]{3,2,1,0:T(8,128)(2,1)S(1)}, bf16[4,4,32,2560]{3,2,1,0:T(8,128)(2,1)}, u32[]{:S(2)}) copy-start(bf16[4,4,32,2560]{3,2,1,0:T(8,128)(2,1)} %get-tuple-element.32) | copy-start | bytes 7864324
  170.5 2.9 copy-start.3
  194.9 0.7 copy-start.4
  194.9 0.7 copy-start.6
  219.5 2.2 copy-start.1
  219.8 58.6 %collective-permute-start.2 = (bf16[4,4,32,2560]{3,2,1,0:T(8,128)(2,1)S(1)}, bf16[4,4,32,2560]{3,2,1,0:T(8,128)(2,1)S(1)}, u32[]{:S(2)}, u32[]{:S(2)}) collective-permute-start(bf16[4,4,32,2560]{3,2,1,0:T(8,128)(2,1)S(1)} %broadcast_select_fusion.3), channel_id=1, source_target_pairs={{0,1},{1,0},{2,3},{3,2},{4,5},{5,4},{6,7},{7,6},{8,9},{9,8},{10,11... | collective-permute-start | bytes 7864328 | tf_op jit(solution)/shard_map/ppermute | solution.py:16
  223.3 3.1 collective-permute-start.7
  226.3 4.2 %collective-permute-start.8 = (f32[2560]{0:T(1024)S(1)}, f32[2560]{0:T(1024)S(1)}, u32[]{:S(2)}, u32[]{:S(2)}) collective-permute-start(f32[2560]{0:T(1024)S(1)} %add.202), channel_id=1, source_target_pairs={{0,4},{2,6},{4,0},{6,2},{1,5},{3,7},{5,1},{7,3},{8,12},{10,14},{12... | collective-permute-start | bytes 30728 | tf_op jit(solution)/shard_map/ppermute | solution.py:16
  230.6 3.7 collective-permute-start.9
  234.3 4.7 %collective-permute-start.10 = (f32[2560]{0:T(1024)S(1)}, f32[2560]{0:T(1024)S(1)}, u32[]{:S(2)}, u32[]{:S(2)}) collective-permute-start(f32[2560]{0:T(1024)S(1)} %add.204), channel_id=1, source_target_pairs={{0,16},{8,24},{16,0},{24,8},{1,17},{9,25},{17,1},{25,9},{2,18},{10... | collective-permute-start | bytes 30728 | tf_op jit(solution)/shard_map/ppermute | solution.py:16
Sparse Core Ops, SparseCore 0:
  9.6 96.0 all-gather.1
  195.1 191.3 reduce-scatter.1
where the time goes:
time: 396 us
  waiting for transfers between devices  251 us (63%)
  matrix products  72 us (18%)
  starting transfers between devices  24.7 us (6%)
  other arithmetic  23.3 us (6%)
  between operations  15 us (4%)
  local copies, waits for them, and re-layouts  10.7 us (3%)
    ppermute x7, waiting for transfers between devices, swap(): return lax.ppermute(value, axis, [(i, i ^ distance) for i in range(count)])  114 us
    reduce_scatter x1, waiting for transfers between devices, shards(): lax.psum_scatter(weight_term, ('dp', 'tile'), scatter_dimension=0, tiled=...  104 us
    all_gather x1, waiting for transfers between devices, shards(): full_weight = lax.all_gather(weight, ('dp', 'tile'), axis=0, tiled=True)  29.9 us
    dot_general x1, matrix products, shards(): lax.dot_general(flat_grad, full_weight, (((1,), (1,)), ((), ())), preferr...  26.6 us
    dot_general x1, matrix products, shards(): output = jnp.dot(columns, full_weight, preferred_element_type=jnp.float32)  23.9 us
    dot_general x1, matrix products, shards(): lax.dot_general(columns, flat_grad, (((0,), (0,)), ((), ())), preferred_e...  21.5 us
    ppermute x7, starting transfers between devices, swap(): return lax.ppermute(value, axis, [(i, i ^ distance) for i in range(count)])  14.9 us
    select_n x4, other arithmetic, pick(): result = jnp.where(index == place, pieces[place], result)  8.58 us
  transfers between devices with their start and end apart: 13, of which 11 were waited for; matrix products, arithmetic and copies ran while one was open for 10% of the time, Pallas kernels for 0%

commit v1 on v0

--- a/solution.py
+++ b/solution.py
@@ -75,7 +75,18 @@
         weight_term, ("dp", "tile"), scatter_dimension=0, tiled=True
     ).astype(jnp.float32)
     grad_bias = sum_over(jnp.sum(flat_grad, axis=0, dtype=jnp.float32), ("tile", "dp"))
-    full_weight = lax.all_gather(weight, ("dp", "tile"), axis=0, tiled=True)
+    ways = lax.axis_size(("dp", "tile"))
+    up = [(d, (d + 1) % ways) for d in range(ways)]
+    down = [(d, (d - 1) % ways) for d in range(ways)]
+    earlier, later = ([weight], [weight])
+    for _ in range(ways // 2):
+        earlier.append(lax.ppermute(earlier[-1], ("dp", "tile"), up))
+    for _ in range((ways - 1) // 2):
+        later.append(lax.ppermute(later[-1], ("dp", "tile"), down))
+    line = jnp.concatenate([*earlier[::-1], *later[1:]], axis=0)
+    full_weight = jnp.roll(
+        line, (lax.axis_index(("dp", "tile")) - ways // 2) * weight.shape[0], axis=0
+    )
     output = jnp.dot(columns, full_weight, preferred_element_type=jnp.float32)
     tokens = (
         (output.reshape(frame_count, row_count, col_count, share) + bias.astype(jnp.float32))

time: 396 us -> 555 us (1.40)
  starting transfers between devices: 24.7 us -> 155 us
  local copies, waits for them, and re-layouts: 10.7 us -> 67.3 us
  waiting for transfers between devices: 251 us -> 218 us
    ppermute x0 -> x15, starting transfers between devices: none -> 114 us  [the longest x8 109 us: shards(): earlier.append(lax.ppermute(earlier[-1], ('dp', 'tile'), up))]
    ppermute x7, waiting for transfers between devices: 114 us -> 58.4 us  [swap(): return lax.ppermute(value, axis, [(i, i ^ distance) for i in range(count)])]
    unnamed x22 -> x89, local copies, waits for them, and re-layouts: 5.02 us -> 59.7 us
    ppermute x0 -> x15, waiting for transfers between devices: none -> 51.6 us  [the longest x8 51.6 us: shards(): earlier.append(lax.ppermute(earlier[-1], ('dp', 'tile'), up))]
    all_gather x1 -> x0, waiting for transfers between devices: 29.9 us -> none  [shards(): full_weight = lax.all_gather(weight, ('dp', 'tile'), axis=0, tiled=True)]
    ppermute x2, starting transfers between devices: 7.15 us -> 27.9 us  [neighbours(): lax.ppermute(high_row, axis, forward)]
  transfers between devices with their start and end apart: 13 -> 27, of which waited for: 11 -> 15; matrix products, arithmetic and copies ran while one was open for 10% -> 11% of each run, Pallas kernels for 0% -> 0%
where the time goes in v1:
time: 555 us; the launch traced here: 554 us
  waiting for transfers between devices  218 us (39%)
  starting transfers between devices  155 us (28%)
  matrix products  74.5 us (13%)
  local copies, waits for them, and re-layouts  67.3 us (12%)
  other arithmetic  23.3 us (4%)
  between operations  15 us (3%)
    ppermute x8, starting transfers between devices, shards(): earlier.append(lax.ppermute(earlier[-1], ('dp', 'tile'), up))  109 us
    reduce_scatter x1, waiting for transfers between devices, shards(): lax.psum_scatter(weight_term, ('dp', 'tile'), scatter_dimension=0, tiled=...  103 us
    unnamed x89, local copies, waits for them, and re-layouts  59.7 us
    ppermute x7, waiting for transfers between devices, swap(): return lax.ppermute(value, axis, [(i, i ^ distance) for i in range(count)])  58.4 us
    ppermute x8, waiting for transfers between devices, shards(): earlier.append(lax.ppermute(earlier[-1], ('dp', 'tile'), up))  51.6 us
    ppermute x2, starting transfers between devices, neighbours(): lax.ppermute(high_row, axis, forward)  27.9 us
    dot_general x1, matrix products, shards(): lax.dot_general(flat_grad, full_weight, (((1,), (1,)), ((), ())), preferr...  25.8 us
    dot_general x1, matrix products, shards(): lax.dot_general(columns, flat_grad, (((0,), (0,)), ((), ())), preferred_e...  24.6 us
  transfers between devices with their start and end apart: 27, of which 15 were waited for; matrix products, arithmetic and copies ran while one was open for 11% of the time, Pallas kernels for 0%

profile of v1, /device:TPU:0, one launch (start us, length us, event | category | flops | bytes accessed | tf_op | source)
XLA Modules:
  0.0 553.8 jit_solution(15807133512378389880)
XLA Ops:
  7.7 18.3 %collective-permute-done.2 = bf16[216,2560]{1,0:T(8,128)(2,1)S(1)} collective-permute-done((bf16[216,2560]{1,0:T(8,128)(2,1)}, bf16[216,2560]{1,0:T(8,128)(2,1)S(1)}, u32[]{:S(2)}, u32[]{:S(2)}) %collective-permute-start.2) | collective-permute-done | bytes 1105952 | tf_op jit(solution)/shard_map/ppermute | solution.py:83
  27.0 4.4 collective-permute-start.10
  31.5 13.2 %collective-permute-done.3 = bf16[216,2560]{1,0:T(8,128)(2,1)S(1)} collective-permute-done((bf16[216,2560]{1,0:T(8,128)(2,1)S(1)}, bf16[216,2560]{1,0:T(8,128)(2,1)S(1)}, u32[]{:S(2)}, u32[]{:S(2)}) %collective-permute-start.3) | collective-permute-done | bytes 1105952 | tf_op jit(solution)/shard_map/ppermute | solution.py:83
  44.7 5.9 %collective-permute-start.4 = (bf16[216,2560]{1,0:T(8,128)(2,1)S(1)}, bf16[216,2560]{1,0:T(8,128)(2,1)S(1)}, u32[]{:S(2)}, u32[]{:S(2)}) collective-permute-start(bf16[216,2560]{1,0:T(8,128)(2,1)S(1)} %collective-permute-done.3), channel_id=1, source_target_pairs={{0,2},{2,4},{4,6},{6,8},{8,10},{10,12},{12,14},{14,16},{16,18},{18... | collective-permute-start | bytes 3317768 | tf_op jit(solution)/shard_map/ppermute | solution.py:83
  50.7 11.6 %collective-permute-done.4 = bf16[216,2560]{1,0:T(8,128)(2,1)S(1)} collective-permute-done((bf16[216,2560]{1,0:T(8,128)(2,1)S(1)}, bf16[216,2560]{1,0:T(8,128)(2,1)S(1)}, u32[]{:S(2)}, u32[]{:S(2)}) %collective-permute-start.4) | collective-permute-done | bytes 1105952 | tf_op jit(solution)/shard_map/ppermute | solution.py:83
  62.3 14.3 %collective-permute-start.5 = (bf16[216,2560]{1,0:T(8,128)(2,1)S(1)}, bf16[216,2560]{1,0:T(8,128)(2,1)}, u32[]{:S(2)}, u32[]{:S(2)}) collective-permute-start(bf16[216,2560]{1,0:T(8,128)(2,1)S(1)} %collective-permute-done.4), channel_id=1, source_target_pairs={{0,2},{2,4},{4,6},{6,8},{8,10},{10,12},{12,14},{14,16},{16,18},{18... | collective-permute-start | bytes 3317768 | tf_op jit(solution)/shard_map/ppermute | solution.py:83
  76.6 4.7 collective-permute-done.5
  81.2 21.3 %collective-permute-start.6 = (bf16[216,2560]{1,0:T(8,128)(2,1)}, bf16[216,2560]{1,0:T(8,128)(2,1)S(1)}, u32[]{:S(2)}, u32[]{:S(2)}) collective-permute-start(bf16[216,2560]{1,0:T(8,128)(2,1)} %collective-permute-done.5), channel_id=1, source_target_pairs={{0,2},{2,4},{4,6},{6,8},{8,10},{10,12},{12,14},{14,16},{16,18},{18... | collective-permute-start | bytes 3317768 | tf_op jit(solution)/shard_map/ppermute | solution.py:83
  102.5 4.3 broadcast_select_fusion.1
  106.8 1.5 collective-permute-start.18
  109.4 20.2 %collective-permute-start.7 = (bf16[216,2560]{1,0:T(8,128)(2,1)S(1)}, bf16[216,2560]{1,0:T(8,128)(2,1)S(1)}, u32[]{:S(2)}, u32[]{:S(2)}) collective-permute-start(bf16[216,2560]{1,0:T(8,128)(2,1)S(1)} %collective-permute-done.6), channel_id=1, source_target_pairs={{0,2},{2,4},{4,6},{6,8},{8,10},{10,12},{12,14},{14,16},{16,18},{18... | collective-permute-start | bytes 3317768 | tf_op jit(solution)/shard_map/ppermute | solution.py:83
  130.6 1.4 collective-permute-done.7
  132.0 24.2 %collective-permute-start.8 = (bf16[216,2560]{1,0:T(8,128)(2,1)S(1)}, bf16[216,2560]{1,0:T(8,128)(2,1)}, u32[]{:S(2)}, u32[]{:S(2)}) collective-permute-start(bf16[216,2560]{1,0:T(8,128)(2,1)S(1)} %collective-permute-done.7), channel_id=1, source_target_pairs={{0,2},{2,4},{4,6},{6,8},{8,10},{10,12},{12,14},{14,16},{16,18},{18... | collective-permute-start | bytes 3317768 | tf_op jit(solution)/shard_map/ppermute | solution.py:83
  156.2 2.5 collective-permute-done.8
  158.7 22.6 %collective-permute-start.9 = (bf16[216,2560]{1,0:T(8,128)(2,1)}, bf16[216,2560]{1,0:T(8,128)(2,1)}, u32[]{:S(2)}, u32[]{:S(2)}) collective-permute-start(bf16[216,2560]{1,0:T(8,128)(2,1)} %collective-permute-done.8), channel_id=1, source_target_pairs={{0,2},{2,4},{4,6},{6,8},{8,10},{10,12},{12,14},{14,16},{16,18},{18... | collective-permute-start | bytes 3317768 | tf_op jit(solution)/shard_map/ppermute | solution.py:83
  182.0 3.7 broadcast_select_fusion.4
  185.8 3.4 constant_dynamic-update-slice_fusion.31
  189.2 2.4 constant_dynamic-update-slice_fusion.30
  193.8 2.4 constant_dynamic-update-slice_fusion.27
  196.2 1.1 constant_dynamic-update-slice_fusion.26
  197.3 1.1 constant_dynamic-update-slice_fusion.25
  198.4 1.1 constant_dynamic-update-slice_fusion.24
  199.6 1.1 constant_dynamic-update-slice_fusion.23
  201.7 1.1 constant_dynamic-update-slice_fusion.21
  203.9 1.1 constant_dynamic-update-slice_fusion.19
  205.0 2.4 constant_dynamic-update-slice_fusion.18
  207.4 2.3 constant_dynamic-update-slice_fusion.17
  210.8 2.3 constant_dynamic-update-slice_fusion.15
  213.1 2.3 constant_dynamic-update-slice_fusion.14
  216.5 1.1 constant_dynamic-update-slice_fusion.12
  217.5 2.3 constant_dynamic-update-slice_fusion.11
  219.9 1.1 constant_dynamic-update-slice_fusion.10
  221.0 1.1 constant_dynamic-update-slice_fusion.9
  224.2 1.1 constant_dynamic-update-slice_fusion.6
  225.3 1.1 constant_dynamic-update-slice_fusion.5
  227.5 1.1 constant_dynamic-update-slice_fusion.3
  228.6 2.3 constant_dynamic-update-slice_fusion.2
  231.0 2.3 constant_dynamic-update-slice_fusion.1
  234.3 25.8 %fusion = f32[8,4,32,3456]{3,2,1,0:T(8,128)} fusion(bf16[6912,2560]{1,0:T(8,128)(2,1)} %constant_dynamic-update-slice_fusion, s32[]{:T(128)S(6)} %select_n.54, bf16[4,4,32,2560]{3,2,1,0:T(8,128)(2,1)S(1)} %get-tuple-element.32, bf16[4,4,32,2560]{3,2,1,0:T(8,128)(2,1)S(1)} %get-tuple-element.31, bf16[8]{0:T(256)(128)(2,1)S(1)} %fusion.30), kind=kOutput, calls=%fused_computation.1 | convolution fusion | flops 18124636160 | bytes 37093396 | tf_op jit(solution)/shard_map/dot_general | solution.py:101
  260.1 5.0 fusion.31
  265.1 3.3 fusion.32
  270.1 23.5 %collective-permute-start.19 = (f32[8,1,32,128]{3,2,1,0:T(8,128)S(1)}, f32[8,1,32,128]{3,2,1,0:T(8,128)S(1)}, u32[]{:S(2)}, u32[]{:S(2)}) collective-permute-start(f32[8,1,32,128]{3,2,1,0:T(8,128)S(1)} %get-tuple-element.35), channel_id=1, source_target_pairs={{0,2},{2,4},{4,6},{1,3},{3,5},{5,7},{8,10},{10,12},{12,14},{9,11},... | collective-permute-start | bytes 393224 | tf_op jit(solution)/shard_map/ppermute | solution.py:41
  293.7 1.3 collective-permute-start.20
  295.1 3.8 collective-permute-done.20
  299.0 1.6 collective-permute-start.21
  300.6 10.6 %collective-permute-done.21 = f32[8,4,32,128]{3,2,1,0:T(8,128)S(1)} collective-permute-done((f32[8,4,32,128]{3,2,1,0:T(8,128)S(1)}, f32[8,4,32,128]{3,2,1,0:T(8,128)S(1)}, u32[]{:S(2)}, u32[]{:S(2)}) %collective-permute-start.21) | collective-permute-done | bytes 524320 | tf_op jit(solution)/shard_map/ppermute | solution.py:16
  312.3 4.4 collective-permute-start
  316.7 1.5 collective-permute-start.1
  318.2 1.6 collective-permute-done.1
  325.7 1.1 slice_dynamic-update-slice_fusion.3
  329.8 24.6 %bitcast_convert_fusion = bf16[3456,2560]{1,0:T(8,128)(2,1)} fusion(bf16[8,4,32,3456]{3,2,1,0:T(8,128)(2,1)} %slice_dynamic-update-slice_fusion, bf16[4,4,32,2560]{3,2,1,0:T(8,128)(2,1)S(1)} %get-tuple-element.32, bf16[4,4,32,2560]{3,2,1,0:T(8,128)(2,1)S(1)} %get-tuple-element.31, bf16[8]{0:T(256)(128)(2,1)S(1)} %fusion.30), kind=kOutput, calls=%fused_computation | convolution fusion | flops 18133483520 | bytes 30015504 | tf_op jit(solution)/shard_map/dot_general | solution.py:71
  355.1 24.1 %multiply_convert_fusion = bf16[8,4,32,2560]{3,2,1,0:T(8,128)(2,1)S(1)} fusion(bf16[8,4,32,3456]{3,2,1,0:T(8,128)(2,1)} %slice_dynamic-update-slice_fusion, bf16[6912,2560]{1,0:T(8,128)(2,1)} %constant_dynamic-update-slice_fusion, s32[]{:T(128)S(6)} %select_n.54, f32[8]{0:T(128)S(1)} %copy-done.24, f32[2560]{0:T(1024)S(1)} %convert_element_type.90), kind=kOutput, calls=%fused_computation.8 | convolution fusion | flops 18127257600 | bytes 30025764 | tf_op jit(solution)/shard_map/dot_general | solution.py:90
  379.5 1.6 collective-permute-start.17
  381.4 1.5 convert_reduce_fusion
  383.0 2.5 collective-permute-start.22
  386.6 3.4 collective-permute-done.23
  390.0 1.3 collective-permute-start.24
  391.3 2.4 collective-permute-done.24
  393.7 2.3 collective-permute-start.25
  396.1 3.6 collective-permute-done.25
  400.3 37.5 %collective-permute-done.17 = bf16[4,4,32,2560]{3,2,1,0:T(8,128)(2,1)S(1)} collective-permute-done((bf16[4,4,32,2560]{3,2,1,0:T(8,128)(2,1)S(1)}, bf16[4,4,32,2560]{3,2,1,0:T(8,128)(2,1)S(1)}, u32[]{:S(2)}, u32[]{:S(2)}) %collective-permute-start.17) | collective-permute-done | bytes 2621472 | tf_op jit(solution)/shard_map/ppermute | solution.py:16
  438.3 3.0 maximum_bitcast_fusion
  441.3 102.8 %reduce-scatter.2.cloned.1.call-done = bf16[216,2560]{1,0:T(8,128)(2,1)} async-done(((bf16[3456,2560]{1,0:T(8,128)(2,1)}), bf16[216,2560]{1,0:T(8,128)(2,1)}) %reduce-scatter.2.cloned.1.call-update) | async-done | bytes 1105936 | tf_op jit(solution)/shard_map/reduce_scatter | solution.py:74
  544.1 2.9 convert_element_type.95
  (114 shorter events, 29.8 us)
Async XLA Ops:
  7.2 537.0 %reduce-scatter.2.cloned.1.call-start = ((), (), s32[]{:S(2)}) async-start(), calls=%async_computation.1 | async-start | bytes 18800640 | tf_op jit(solution)/shard_map/reduce_scatter | solution.py:74
  7.2 18.8 %collective-permute-start.2 = (bf16[216,2560]{1,0:T(8,128)(2,1)}, bf16[216,2560]{1,0:T(8,128)(2,1)S(1)}, u32[]{:S(2)}, u32[]{:S(2)}) collective-permute-start(bf16[216,2560]{1,0:T(8,128)(2,1)} %param.7), channel_id=1, source_target_pairs={{0,2},{2,4},{4,6},{6,8},{8,10},{10,12},{12,14},{14,16},{16,18},{18... | collective-permute-start | bytes 3317768 | tf_op jit(solution)/shard_map/ppermute | solution.py:83
  26.0 1.0 copy-start.3
  27.0 17.6 %collective-permute-start.3 = (bf16[216,2560]{1,0:T(8,128)(2,1)S(1)}, bf16[216,2560]{1,0:T(8,128)(2,1)S(1)}, u32[]{:S(2)}, u32[]{:S(2)}) collective-permute-start(bf16[216,2560]{1,0:T(8,128)(2,1)S(1)} %collective-permute-done.2), channel_id=1, source_target_pairs={{0,2},{2,4},{4,6},{6,8},{8,10},{10,12},{12,14},{14,16},{16,18},{18... | collective-permute-start | bytes 3317768 | tf_op jit(solution)/shard_map/ppermute | solution.py:83
  27.0 23.6 %collective-permute-start.10 = (bf16[216,2560]{1,0:T(8,128)(2,1)}, bf16[216,2560]{1,0:T(8,128)(2,1)S(1)}, u32[]{:S(2)}, u32[]{:S(2)}) collective-permute-start(bf16[216,2560]{1,0:T(8,128)(2,1)} %param.7), channel_id=1, source_target_pairs={{0,30},{2,0},{4,2},{6,4},{8,6},{10,8},{12,10},{14,12},{16,14},{18,... | collective-permute-start | bytes 3317768 | tf_op jit(solution)/shard_map/ppermute | solution.py:85
  44.7 5.9 %copy-start.7 = (bf16[216,2560]{1,0:T(8,128)(2,1)}, bf16[216,2560]{1,0:T(8,128)(2,1)S(1)}, u32[]{:S(2)}) copy-start(bf16[216,2560]{1,0:T(8,128)(2,1)S(1)} %collective-permute-done.3) | copy-start | bytes 3317764
  44.7 17.6 %collective-permute-start.4 = (bf16[216,2560]{1,0:T(8,128)(2,1)S(1)}, bf16[216,2560]{1,0:T(8,128)(2,1)S(1)}, u32[]{:S(2)}, u32[]{:S(2)}) collective-permute-start(bf16[216,2560]{1,0:T(8,128)(2,1)S(1)} %collective-permute-done.3), channel_id=1, source_target_pairs={{0,2},{2,4},{4,6},{6,8},{8,10},{10,12},{12,14},{14,16},{16,18},{18... | collective-permute-start | bytes 3317768 | tf_op jit(solution)/shard_map/ppermute | solution.py:83
  50.6 131.4 %copy-start.5 = (bf16[216,2560]{1,0:T(8,128)(2,1)}, bf16[216,2560]{1,0:T(8,128)(2,1)S(1)}, u32[]{:S(2)}) copy-start(bf16[216,2560]{1,0:T(8,128)(2,1)S(1)} %collective-permute-done.10) | copy-start | bytes 3317764
  50.6 26.0 %collective-permute-start.11 = (bf16[216,2560]{1,0:T(8,128)(2,1)S(1)}, bf16[216,2560]{1,0:T(8,128)(2,1)S(1)}, u32[]{:S(2)}, u32[]{:S(2)}) collective-permute-start(bf16[216,2560]{1,0:T(8,128)(2,1)S(1)} %collective-permute-done.10), channel_id=1, source_target_pairs={{0,30},{2,0},{4,2},{6,4},{8,6},{10,8},{12,10},{14,12},{16,14},{18,... | collective-permute-start | bytes 3317768 | tf_op jit(solution)/shard_map/ppermute | solution.py:85
  62.3 119.7 %copy-start.11 = (bf16[216,2560]{1,0:T(8,128)(2,1)}, bf16[216,2560]{1,0:T(8,128)(2,1)S(1)}, u32[]{:S(2)}) copy-start(bf16[216,2560]{1,0:T(8,128)(2,1)S(1)} %collective-permute-done.4) | copy-start | bytes 3317764
  62.3 18.9 %collective-permute-start.5 = (bf16[216,2560]{1,0:T(8,128)(2,1)S(1)}, bf16[216,2560]{1,0:T(8,128)(2,1)}, u32[]{:S(2)}, u32[]{:S(2)}) collective-permute-start(bf16[216,2560]{1,0:T(8,128)(2,1)S(1)} %collective-permute-done.4), channel_id=1, source_target_pairs={{0,2},{2,4},{4,6},{6,8},{8,10},{10,12},{12,14},{14,16},{16,18},{18... | collective-permute-start | bytes 3317768 | tf_op jit(solution)/shard_map/ppermute | solution.py:83
  76.6 105.4 %copy-start.9 = (bf16[216,2560]{1,0:T(8,128)(2,1)}, bf16[216,2560]{1,0:T(8,128)(2,1)S(1)}, u32[]{:S(2)}) copy-start(bf16[216,2560]{1,0:T(8,128)(2,1)S(1)} %collective-permute-done.11) | copy-start | bytes 3317764
  76.6 31.7 %collective-permute-start.12 = (bf16[216,2560]{1,0:T(8,128)(2,1)S(1)}, bf16[216,2560]{1,0:T(8,128)(2,1)S(1)}, u32[]{:S(2)}, u32[]{:S(2)}) collective-permute-start(bf16[216,2560]{1,0:T(8,128)(2,1)S(1)} %collective-permute-done.11), channel_id=1, source_target_pairs={{0,30},{2,0},{4,2},{6,4},{8,6},{10,8},{12,10},{14,12},{16,14},{18,... | collective-permute-start | bytes 3317768 | tf_op jit(solution)/shard_map/ppermute | solution.py:85
  81.2 28.1 %collective-permute-start.6 = (bf16[216,2560]{1,0:T(8,128)(2,1)}, bf16[216,2560]{1,0:T(8,128)(2,1)S(1)}, u32[]{:S(2)}, u32[]{:S(2)}) collective-permute-start(bf16[216,2560]{1,0:T(8,128)(2,1)} %collective-permute-done.5), channel_id=1, source_target_pairs={{0,2},{2,4},{4,6},{6,8},{8,10},{10,12},{12,14},{14,16},{16,18},{18... | collective-permute-start | bytes 3317768 | tf_op jit(solution)/shard_map/ppermute | solution.py:83
  106.8 75.2 %collective-permute-start.18 = (bf16[4,4,32,2560]{3,2,1,0:T(8,128)(2,1)}, bf16[4,4,32,2560]{3,2,1,0:T(8,128)(2,1)}, u32[]{:S(2)}, u32[]{:S(2)}) collective-permute-start(bf16[4,4,32,2560]{3,2,1,0:T(8,128)(2,1)} %broadcast_select_fusion.1), channel_id=1, source_target_pairs={{0,1},{1,0},{2,3},{3,2},{4,5},{5,4},{6,7},{7,6},{8,9},{9,8},{10,11... | collective-permute-start | bytes 7864328 | tf_op jit(solution)/shard_map/ppermute | solution.py:16
  108.3 1.0 copy-start.13
  109.4 20.2 %collective-permute-start.13 = (bf16[216,2560]{1,0:T(8,128)(2,1)S(1)}, bf16[216,2560]{1,0:T(8,128)(2,1)S(1)}, u32[]{:S(2)}, u32[]{:S(2)}) collective-permute-start(bf16[216,2560]{1,0:T(8,128)(2,1)S(1)} %collective-permute-done.12), channel_id=1, source_target_pairs={{0,30},{2,0},{4,2},{6,4},{8,6},{10,8},{12,10},{14,12},{16,14},{18,... | collective-permute-start | bytes 3317768 | tf_op jit(solution)/shard_map/ppermute | solution.py:85
  109.4 46.8 %copy-start.17 = (bf16[216,2560]{1,0:T(8,128)(2,1)}, bf16[216,2560]{1,0:T(8,128)(2,1)S(1)}, u32[]{:S(2)}) copy-start(bf16[216,2560]{1,0:T(8,128)(2,1)S(1)} %collective-permute-done.6) | copy-start | bytes 3317764
  109.4 22.6 %collective-permute-start.7 = (bf16[216,2560]{1,0:T(8,128)(2,1)S(1)}, bf16[216,2560]{1,0:T(8,128)(2,1)S(1)}, u32[]{:S(2)}, u32[]{:S(2)}) collective-permute-start(bf16[216,2560]{1,0:T(8,128)(2,1)S(1)} %collective-permute-done.6), channel_id=1, source_target_pairs={{0,2},{2,4},{4,6},{6,8},{8,10},{10,12},{12,14},{14,16},{16,18},{18... | collective-permute-start | bytes 3317768 | tf_op jit(solution)/shard_map/ppermute | solution.py:83
  129.6 1.0 copy-start.15
  130.6 25.6 %collective-permute-start.14 = (bf16[216,2560]{1,0:T(8,128)(2,1)S(1)}, bf16[216,2560]{1,0:T(8,128)(2,1)}, u32[]{:S(2)}, u32[]{:S(2)}) collective-permute-start(bf16[216,2560]{1,0:T(8,128)(2,1)S(1)} %collective-permute-done.13), channel_id=1, source_target_pairs={{0,30},{2,0},{4,2},{6,4},{8,6},{10,8},{12,10},{14,12},{16,14},{18,... | collective-permute-start | bytes 3317768 | tf_op jit(solution)/shard_map/ppermute | solution.py:85
  132.0 24.2 %copy-start.19 = (bf16[216,2560]{1,0:T(8,128)(2,1)}, bf16[216,2560]{1,0:T(8,128)(2,1)S(1)}, u32[]{:S(2)}) copy-start(bf16[216,2560]{1,0:T(8,128)(2,1)S(1)} %collective-permute-done.7) | copy-start | bytes 3317764
  132.0 26.7 %collective-permute-start.8 = (bf16[216,2560]{1,0:T(8,128)(2,1)S(1)}, bf16[216,2560]{1,0:T(8,128)(2,1)}, u32[]{:S(2)}, u32[]{:S(2)}) collective-permute-start(bf16[216,2560]{1,0:T(8,128)(2,1)S(1)} %collective-permute-done.7), channel_id=1, source_target_pairs={{0,2},{2,4},{4,6},{6,8},{8,10},{10,12},{12,14},{14,16},{16,18},{18... | collective-permute-start | bytes 3317768 | tf_op jit(solution)/shard_map/ppermute | solution.py:83
  156.2 29.5 %collective-permute-start.15 = (bf16[216,2560]{1,0:T(8,128)(2,1)}, bf16[216,2560]{1,0:T(8,128)(2,1)}, u32[]{:S(2)}, u32[]{:S(2)}) collective-permute-start(bf16[216,2560]{1,0:T(8,128)(2,1)} %collective-permute-done.14), channel_id=1, source_target_pairs={{0,30},{2,0},{4,2},{6,4},{8,6},{10,8},{12,10},{14,12},{16,14},{18,... | collective-permute-start | bytes 3317768 | tf_op jit(solution)/shard_map/ppermute | solution.py:85
  158.7 27.1 %collective-permute-start.9 = (bf16[216,2560]{1,0:T(8,128)(2,1)}, bf16[216,2560]{1,0:T(8,128)(2,1)}, u32[]{:S(2)}, u32[]{:S(2)}) collective-permute-start(bf16[216,2560]{1,0:T(8,128)(2,1)} %collective-permute-done.8), channel_id=1, source_target_pairs={{0,2},{2,4},{4,6},{6,8},{8,10},{10,12},{12,14},{14,16},{16,18},{18... | collective-permute-start | bytes 3317768 | tf_op jit(solution)/shard_map/ppermute | solution.py:83
  182.0 9.6 %copy-start.20 = (bf16[216,2560]{1,0:T(8,128)(2,1)S(1)}, bf16[216,2560]{1,0:T(8,128)(2,1)}, u32[]{:S(2)}) copy-start(bf16[216,2560]{1,0:T(8,128)(2,1)} %copy-done.19) | copy-start | bytes 3317764
  182.0 10.7 %copy-start.18 = (bf16[216,2560]{1,0:T(8,128)(2,1)S(1)}, bf16[216,2560]{1,0:T(8,128)(2,1)}, u32[]{:S(2)}) copy-start(bf16[216,2560]{1,0:T(8,128)(2,1)} %copy-done.17) | copy-start | bytes 3317764
  185.7 144.1 %copy-start = (bf16[4,4,32,2560]{3,2,1,0:T(8,128)(2,1)}, bf16[4,4,32,2560]{3,2,1,0:T(8,128)(2,1)S(1)}, u32[]{:S(2)}) copy-start(bf16[4,4,32,2560]{3,2,1,0:T(8,128)(2,1)S(1)} %get-tuple-element.32) | copy-start | bytes 7864324
  185.7 10.5 %copy-start.12 = (bf16[216,2560]{1,0:T(8,128)(2,1)S(1)}, bf16[216,2560]{1,0:T(8,128)(2,1)}, u32[]{:S(2)}) copy-start(bf16[216,2560]{1,0:T(8,128)(2,1)} %copy-done.11) | copy-start | bytes 3317764
  185.7 11.6 %copy-start.8 = (bf16[216,2560]{1,0:T(8,128)(2,1)S(1)}, bf16[216,2560]{1,0:T(8,128)(2,1)}, u32[]{:S(2)}) copy-start(bf16[216,2560]{1,0:T(8,128)(2,1)} %copy-done.7) | copy-start | bytes 3317764
  185.7 23.9 %collective-permute-start.16 = (bf16[216,2560]{1,0:T(8,128)(2,1)}, bf16[216,2560]{1,0:T(8,128)(2,1)S(1)}, u32[]{:S(2)}, u32[]{:S(2)}) collective-permute-start(bf16[216,2560]{1,0:T(8,128)(2,1)} %collective-permute-done.15), channel_id=1, source_target_pairs={{0,30},{2,0},{4,2},{6,4},{8,6},{10,8},{12,10},{14,12},{16,14},{18,... | collective-permute-start | bytes 3317768 | tf_op jit(solution)/shard_map/ppermute | solution.py:85
  189.2 9.2 %copy-start.4 = (bf16[216,2560]{1,0:T(8,128)(2,1)S(1)}, bf16[216,2560]{1,0:T(8,128)(2,1)}, u32[]{:S(2)}) copy-start(bf16[216,2560]{1,0:T(8,128)(2,1)} %copy-done.3) | copy-start | bytes 3317764
  191.6 7.9 %copy-start.2 = (bf16[216,2560]{1,0:T(8,128)(2,1)S(1)}, bf16[216,2560]{1,0:T(8,128)(2,1)}, u32[]{:S(2)}) copy-start(bf16[216,2560]{1,0:T(8,128)(2,1)} %param.7) | copy-start | bytes 3317764
  192.7 8.0 %copy-start.6 = (bf16[216,2560]{1,0:T(8,128)(2,1)S(1)}, bf16[216,2560]{1,0:T(8,128)(2,1)}, u32[]{:S(2)}) copy-start(bf16[216,2560]{1,0:T(8,128)(2,1)} %copy-done.5) | copy-start | bytes 3317764
  193.8 8.0 %copy-start.10 = (bf16[216,2560]{1,0:T(8,128)(2,1)S(1)}, bf16[216,2560]{1,0:T(8,128)(2,1)}, u32[]{:S(2)}) copy-start(bf16[216,2560]{1,0:T(8,128)(2,1)} %copy-done.9) | copy-start | bytes 3317764
  196.2 6.7 %copy-start.14 = (bf16[216,2560]{1,0:T(8,128)(2,1)S(1)}, bf16[216,2560]{1,0:T(8,128)(2,1)}, u32[]{:S(2)}) copy-start(bf16[216,2560]{1,0:T(8,128)(2,1)} %copy-done.13) | copy-start | bytes 3317764
  197.3 6.6 %copy-start.16 = (bf16[216,2560]{1,0:T(8,128)(2,1)S(1)}, bf16[216,2560]{1,0:T(8,128)(2,1)}, u32[]{:S(2)}) copy-start(bf16[216,2560]{1,0:T(8,128)(2,1)} %copy-done.15) | copy-start | bytes 3317764
  268.8 42.4 %copy-start.21 = (bf16[1,8,4,32,128]{4,3,2,1,0:T(8,128)(2,1)S(1)}, bf16[1,8,4,32,128]{4,3,2,1,0:T(8,128)(2,1)}, u32[]{:S(2)}) copy-start(bf16[1,8,4,32,128]{4,3,2,1,0:T(8,128)(2,1)} %param.5) | copy-start | bytes 786436
  270.1 24.9 %collective-permute-start.19 = (f32[8,1,32,128]{3,2,1,0:T(8,128)S(1)}, f32[8,1,32,128]{3,2,1,0:T(8,128)S(1)}, u32[]{:S(2)}, u32[]{:S(2)}) collective-permute-start(f32[8,1,32,128]{3,2,1,0:T(8,128)S(1)} %get-tuple-element.35), channel_id=1, source_target_pairs={{0,2},{2,4},{4,6},{1,3},{3,5},{5,7},{8,10},{10,12},{12,14},{9,11},... | collective-permute-start | bytes 393224 | tf_op jit(solution)/shard_map/ppermute | solution.py:41
  293.7 5.2 collective-permute-start.20
  299.0 12.2 %collective-permute-start.21 = (f32[8,4,32,128]{3,2,1,0:T(8,128)S(1)}, f32[8,4,32,128]{3,2,1,0:T(8,128)S(1)}, u32[]{:S(2)}, u32[]{:S(2)}) collective-permute-start(f32[8,4,32,128]{3,2,1,0:T(8,128)S(1)} %slice_add_fusion), channel_id=1, source_target_pairs={{0,1},{1,0},{2,3},{3,2},{4,5},{5,4},{6,7},{7,6},{8,9},{9,8},{10,11... | collective-permute-start | bytes 1572872 | tf_op jit(solution)/shard_map/ppermute | solution.py:16
  300.6 16.1 %copy-start.23 = (f32[8]{0:T(128)}, f32[8]{0:T(128)S(1)}, u32[]{:S(2)}) copy-start(f32[8]{0:T(128)S(1)} %compare_convert_fusion) | copy-start | bytes 100
  312.3 5.9 %collective-permute-start = (bf16[8,1,32,128]{3,2,1,0:T(8,128)(2,1)S(1)}, bf16[8,1,32,128]{3,2,1,0:T(8,128)(2,1)S(1)}, u32[]{:S(2)}, u32[]{:S(2)}) collective-permute-start(bf16[8,1,32,128]{3,2,1,0:T(8,128)(2,1)S(1)} %get-tuple-element.42), channel_id=1, source_target_pairs={{0,2},{2,4},{4,6},{1,3},{3,5},{5,7},{8,10},{10,12},{12,14},{9,11},... | collective-permute-start | bytes 196616 | tf_op jit(solution)/shard_map/ppermute | solution.py:41
  316.7 3.1 collective-permute-start.1
  354.4 0.7 copy-start.22
  354.4 0.7 copy-start.24
  379.3 2.2 copy-start.1
  379.5 58.3 %collective-permute-start.17 = (bf16[4,4,32,2560]{3,2,1,0:T(8,128)(2,1)S(1)}, bf16[4,4,32,2560]{3,2,1,0:T(8,128)(2,1)S(1)}, u32[]{:S(2)}, u32[]{:S(2)}) collective-permute-start(bf16[4,4,32,2560]{3,2,1,0:T(8,128)(2,1)S(1)} %broadcast_select_fusion.3), channel_id=1, source_target_pairs={{0,1},{1,0},{2,3},{3,2},{4,5},{5,4},{6,7},{7,6},{8,9},{9,8},{10,11... | collective-permute-start | bytes 7864328 | tf_op jit(solution)/shard_map/ppermute | solution.py:16
  383.0 3.4 collective-permute-start.22
  386.3 3.7 collective-permute-start.23
  390.0 3.7 collective-permute-start.24
  393.7 6.0 %collective-permute-start.25 = (f32[2560]{0:T(1024)S(1)}, f32[2560]{0:T(1024)S(1)}, u32[]{:S(2)}, u32[]{:S(2)}) collective-permute-start(f32[2560]{0:T(1024)S(1)} %add.221), channel_id=1, source_target_pairs={{0,16},{8,24},{16,0},{24,8},{1,17},{9,25},{17,1},{25,9},{2,18},{10... | collective-permute-start | bytes 30728 | tf_op jit(solution)/shard_map/ppermute | solution.py:16
Sparse Core Ops, SparseCore 0:
  354.6 189.5 reduce-scatter.1
